TPU v7x, 32 devices: a whole 2x2x4 slice. The times are simulated.
32 devices in a mesh: grp: 4 (over z), row: 8 (over y, x, core).
Axes of the slice: x: 2, y: 2, z: 4, core: 2. Of those that a mesh axis runs over, the one named last changes fastest.
Arguments:
- embeddings: bfloat16 [32768, 256], P(('grp', 'row')), may hold values from -6 to 6
- neighbour_tile_mask: int32 [128, 8, 256, 256], P(('grp', 'row')), may hold values 0 or 1
- column_blocks: int32 [128, 8], P(('grp', 'row')), may hold values from 0 to 31, as said below
- seed_labels: int32 [32768], P(('grp', 'row')), may hold values from 0 to 64, as said below
Outputs:
- label_scores: float32 [64, 32768], P(None, ('grp', 'row'))
Inputs may be any that keep to these rules, and one draw needn't show every extreme that they name: `column_blocks`: entry [r, k] names a block of r's group (r // 32) by its index in that group; block b of a group lies on the group's device b // 4 along row. The 8 column blocks of one row-block lie on 8 different devices and never include r itself, so a device receives at most 4 mirrored tiles from one device, at most one from each of its row-blocks; in every draw each device has a device that receives exactly 4 from it. `seed_labels`: 64 marks a node without a seed label.
All inputs are finite; a program needn't handle non-finite values. No bound on the sum of `neighbour_tile_mask` on one device may be relied on, other than what follows from the above.
Results may differ from a plain program's by a relative error of at most 0.00041.
Values may be sent and summed in bfloat16 or wider, within the bound.
A program may use at most 128 MiB of HBM per device.

v0:
```python
import jax
import jax.numpy as jnp
from jax import lax
from jax.sharding import PartitionSpec as P

CLASSES = 64
STEPS = 2


SOFTMAX_WARMTH = 0.1
PROPAGATION = 0.9


def local(embeddings, neighbour_tile_mask, column_blocks, seed_labels):
    blocks_here = neighbour_tile_mask.shape[0]
    tile_edge = neighbour_tile_mask.shape[2]
    graph_breadth = embeddings.shape[1]
    peer_count = lax.axis_size("row")
    node_total = embeddings.shape[0] * peer_count * lax.axis_size("grp")
    features = embeddings.astype(jnp.float32)
    unit_rows = (
        features * lax.rsqrt(jnp.mean(features * features, axis=1, keepdims=True) + 1e-06)
    ).astype(jnp.bfloat16)
    group_units = lax.all_gather(unit_rows, "row", axis=0, tiled=True)
    group_units = group_units.reshape(peer_count * blocks_here, tile_edge, graph_breadth)
    column_units = group_units[column_blocks]
    score_values = jnp.einsum(
        "jie,jkbe->jkib",
        unit_rows.reshape(blocks_here, tile_edge, graph_breadth),
        column_units,
        preferred_element_type=jnp.float32,
    )
    affinity_matrix = jnp.where(
        neighbour_tile_mask > 0, jnp.exp(score_values / (graph_breadth * SOFTMAX_WARMTH)), 0.0
    ).astype(jnp.bfloat16)
    row_sums = jnp.sum(affinity_matrix, axis=(1, 3), dtype=jnp.float32)
    destination = column_blocks // blocks_here
    target = column_blocks % blocks_here
    one_hot = destination[:, :, None] == jnp.arange(peer_count, dtype=jnp.int32)
    slot_target = jnp.sum(jnp.where(one_hot, target[:, :, None] + 1, 0), axis=1).T - 1
    local_index = jnp.arange(blocks_here, dtype=jnp.int32)
    outgoing = jnp.einsum(
        "jkd,jkab->djab",
        one_hot.astype(jnp.bfloat16),
        affinity_matrix,
        preferred_element_type=jnp.float32,
    ).astype(jnp.bfloat16)
    mirrored, arrived = (
        lax.all_to_all(outgoing, "row", split_axis=0, concat_axis=0, tiled=True),
        lax.all_to_all(slot_target, "row", split_axis=0, concat_axis=0, tiled=True),
    )
    column_sums = jnp.sum(mirrored, axis=2, dtype=jnp.float32)
    select_rows = (arrived[:, :, None] == local_index).astype(jnp.float32)
    mirror_degree = jnp.einsum(
        "pjt,pjb->tb", select_rows, column_sums, precision=lax.Precision.HIGHEST
    )
    degree = (1.0 + row_sums + mirror_degree).reshape(-1)
    inverse_root = lax.rsqrt(degree)
    select_bf = select_rows.astype(jnp.bfloat16)
    class_hits = (seed_labels[None, :] == jnp.arange(CLASSES, dtype=jnp.int32)[:, None]).astype(
        jnp.float32
    )
    counts = lax.psum(jnp.sum(class_hits, axis=1), ("grp", "row"))
    seed_field = class_hits * (node_total / (counts + 1.0))[:, None]
    label_field = seed_field
    for iteration in range(STEPS):
        spread = (label_field * inverse_root[None, :]).astype(jnp.bfloat16)
        group_spread = lax.all_gather(spread, "row", axis=1, tiled=True)
        group_spread = group_spread.reshape(CLASSES, peer_count * blocks_here, tile_edge)
        column_spread = group_spread[:, column_blocks]
        forward = jnp.einsum(
            "jkib,cjkb->cji", affinity_matrix, column_spread, preferred_element_type=jnp.float32
        )
        source_spread = group_spread.reshape(CLASSES, peer_count, blocks_here, tile_edge)
        partial_terms = jnp.einsum(
            "pjab,cpja->pjcb", mirrored, source_spread, preferred_element_type=jnp.float32
        ).astype(jnp.bfloat16)
        mirror = jnp.einsum(
            "pjt,pjcb->ctb", select_bf, partial_terms, preferred_element_type=jnp.float32
        )
        summed = (forward + mirror).reshape(CLASSES, -1) + spread.astype(jnp.float32)
        label_field = (
            PROPAGATION * inverse_root[None, :] * summed + (1.0 - PROPAGATION) * seed_field
        )
    return label_field


def solution(mesh):
    return jax.shard_map(
        local,
        mesh=mesh,
        in_specs=(
            P(("grp", "row"), None),
            P(("grp", "row"), None, None, None),
            P(("grp", "row"), None),
            P(("grp", "row")),
        ),
        out_specs=P(None, ("grp", "row")),
        check_vma=False,
    )
```

profile of v0, /device:TPU:0, one launch (start us, length us, event | category | flops | bytes accessed | tf_op | source)
XLA Modules:
  0.0 240.6 jit_solution(8216734506895796542)
XLA Ops:
  6.5 0.0 all-gather.4.cloned.1.call-start
  6.5 1.3 fusion.8
  7.8 2.0 fusion.9
  9.8 0.0 all-gather.4.cloned.1.call-update
  9.9 0.7 fusion.29
  10.6 0.1 select_reduce_fusion
  10.7 0.7 copy.69
  11.4 5.2 %all-to-all-start = ((s32[8,1,4]{2,1,0:T(1,128)}), s32[8,1,4]{2,1,0:T(1,128)S(1)}, u32[]{:S(2)}, u32[]{:S(2)}) async-start(s32[8,1,4]{2,1,0:T(1,128)} %copy.69), calls=%async_computation | async-start | bytes 8192 | tf_op jit(solution)/shard_map/all_to_all | solution.py:50
  16.6 0.1 reshape.55
  16.6 8.8 %copy.68 = s32[4,8,256,256]{2,3,1,0:T(8,128)} copy(s32[4,8,256,256]{3,2,1,0:T(8,128)} %param.5) | data formatting | bytes 16777216 | tf_op args[1]
  25.5 24.0 %all-gather.4.cloned.1.call-done = bf16[8192,256]{1,0:T(8,128)(2,1)} async-done(((bf16[1024,256]{1,0:T(8,128)(2,1)}), bf16[8192,256]{1,0:T(8,128)(2,1)}) %all-gather.4.cloned.1.call-update) | async-done | bytes 4194320 | tf_op jit(solution)/shard_map/all_gather | solution.py:24
  49.4 0.0 copy-start.2
  49.4 5.0 %gather_fusion = bf16[32,256,256]{2,1,0:T(8,128)(2,1)} fusion(bf16[32,256,256]{2,1,0:T(8,128)(2,1)} %bitcast.95, s32[1024]{0:T(1024)S(1)} %pad_clamp_fusion), kind=kCustom, calls=%fused_computation | custom fusion | bytes 8388736 | tf_op jit(solution)/shard_map/gather | solution.py:26
  54.4 0.0 copy-done.2
  54.4 7.4 %convert_reduce_fusion.1 = (f32[4,256]{1,0:T(4,128)S(1)}, bf16[4,8,256,256]{2,3,1,0:T(8,128)(2,1)}) fusion(bf16[4,8,256,256]{3,2,1,0:T(8,128)(2,1)} %bitcast.96, bf16[4,256,256,1]{2,1,3,0:T(8,128)(2,1)S(1)} %bitcast.105, s32[4,8,256,256]{2,3,1,0:T(8,128)} %copy.68), kind=kOutput, calls=%fused_computation.6 | convolution fusion | flops 1086323712 | bytes 17305600 | tf_op jit(solution)/shard_map/jie,jkbe->jkib/dot_general | solution.py:27
  61.8 7.8 %copy.71 = bf16[4,8,256,256]{3,1,2,0:T(8,128)(2,1)} copy(bf16[4,8,256,256]{2,3,1,0:T(8,128)(2,1)} %get-tuple-element.9) | data formatting | bytes 8388608 | tf_op jit(solution)/shard_map/convert_element_type | solution.py:35
  69.6 3.4 %convert_bitcast_fusion = bf16[8,4,256,256]{3,0,2,1:T(8,128)(2,1)S(1)} fusion(bf16[4,8,256,256]{3,1,2,0:T(8,128)(2,1)} %copy.71, s32[4,8]{1,0:T(4,128)S(1)} %get-tuple-element.7), kind=kOutput, calls=%fused_computation.7 | convolution fusion | flops 35651840 | bytes 8388736 | tf_op jit(solution)/shard_map/jkd,jkab->djab/dot_general | solution.py:42
  73.1 2.9 %copy.72 = bf16[8,4,256,256]{3,2,1,0:T(8,128)(2,1)} copy(bf16[8,4,256,256]{3,0,2,1:T(8,128)(2,1)S(1)} %convert_bitcast_fusion) | data formatting | bytes 8388608 | tf_op jit(solution)/shard_map/convert_element_type | solution.py:47
  76.0 0.0 copy-start.3
  76.0 0.0 all-to-all-done
  76.0 4.7 %all-to-all-start.1 = ((bf16[8,4,256,256]{3,2,1,0:T(8,128)(2,1)}), bf16[8,4,256,256]{3,2,1,0:T(8,128)(2,1)}, u32[]{:S(2)}, u32[]{:S(2)}) async-start(bf16[8,4,256,256]{3,2,1,0:T(8,128)(2,1)} %copy.72), calls=%async_computation.1 | async-start | bytes 8388608 | tf_op jit(solution)/shard_map/all_to_all | solution.py:49
  80.6 0.0 all-gather.6.cloned.1.call-start
  80.7 0.0 copy-done.3
  80.7 0.1 convert_reduce_fusion.2
  80.8 82.0 %psum.7 = f32[64]{0:T(128)S(1)} all-reduce(f32[64]{0:T(128)S(1)} %convert_reduce_fusion.2), channel_id=1, replica_groups=mesh['grp'=4,'row'=8] {'grp','row'}, use_global_device_ids=true, to_apply=%region_5.6 | all-reduce | flops 64 | bytes 512 | tf_op jit(solution)/shard_map/psum | solution.py:63
  162.9 0.1 copy.70
  162.9 0.0 all-to-all-done.1
  162.9 2.9 %convert_reduce_fusion = f32[8,4,256]{2,1,0:T(4,128)S(1)} fusion(bf16[8,4,256,256]{3,2,1,0:T(8,128)(2,1)} %all-to-all-done.1), kind=kLoop, calls=%fused_computation.5 | loop fusion | flops 4186112 | bytes 4227072 | tf_op jit(solution)/shard_map/reduce_sum | solution.py:52
  165.8 0.2 fusion.7
  166.0 0.8 fusion.18
  166.8 0.0 all-gather.6.cloned.1.call-update
  166.8 0.2 all-gather.8.cloned.1.call-start
  167.1 22.4 %all-gather.6.cloned.1.call-done = bf16[64,8192]{1,0:T(8,128)(2,1)} async-done(((bf16[64,1024]{1,0:T(8,128)(2,1)}), bf16[64,8192]{1,0:T(8,128)(2,1)}) %all-gather.6.cloned.1.call-update) | async-done | bytes 1048592 | tf_op jit(solution)/shard_map/all_gather | solution.py:68
  189.5 1.8 reshape_reshape.6
  191.3 0.0 copy-start
  191.3 3.3 %convolution_convert_fusion.1 = bf16[8,4,64,256]{3,2,1,0:T(8,128)(2,1)S(1)} fusion(bf16[8,4,256,256]{3,2,1,0:T(8,128)(2,1)} %all-to-all-done.1, bf16[64,8,4,256]{3,2,1,0:T(4,128)(2,1)S(1)} %reshape_reshape.6), kind=kOutput, calls=%fused_computation.9 | convolution fusion | flops 268959744 | bytes 6291456 | tf_op jit(solution)/shard_map/pjab,cpja->pjcb/dot_general | solution.py:75
  194.6 0.7 convolution_bitcast_fusion.2
  195.3 0.0 copy-done
  195.3 0.1 copy.114
  195.4 0.6 gather_fusion.1
  196.0 3.0 %fusion.4 = f32[4,8,8,256]{3,2,1,0:T(8,128)S(1)} fusion(bf16[64,4,8,256]{3,0,2,1:T(8,128)(2,1)S(1)} %bitcast.102, bf16[4,8,256,256]{2,3,1,0:T(8,128)(2,1)} %get-tuple-element.9, f32[64,256,4]{1,2,0:T(4,128)S(1)} %convolution_bitcast_fusion.2), kind=kOutput, calls=%fused_computation.19 | convolution fusion | flops 268500992 | bytes 5767168 | tf_op jit(solution)/shard_map/jkib,cjkb->cji/dot_general | solution.py:71
  199.1 0.8 fusion.17
  199.9 0.0 all-gather.8.cloned.1.call-update
  199.9 23.6 %all-gather.8.cloned.1.call-done = bf16[64,8192]{1,0:T(8,128)(2,1)} async-done(((bf16[64,1024]{1,0:T(8,128)(2,1)}), bf16[64,8192]{1,0:T(8,128)(2,1)}) %all-gather.8.cloned.1.call-update) | async-done | bytes 1048592 | tf_op jit(solution)/shard_map/all_gather | solution.py:68
  223.6 1.8 reshape_reshape.7
  225.4 0.0 copy-start.1
  225.4 3.3 %convolution_convert_fusion = bf16[8,4,64,256]{3,2,1,0:T(8,128)(2,1)S(1)} fusion(bf16[8,4,256,256]{3,2,1,0:T(8,128)(2,1)} %all-to-all-done.1, bf16[64,8,4,256]{3,2,1,0:T(4,128)(2,1)S(1)} %reshape_reshape.7), kind=kOutput, calls=%fused_computation.8 | convolution fusion | flops 268959744 | bytes 6291456 | tf_op jit(solution)/shard_map/pjab,cpja->pjcb/dot_general | solution.py:75
  228.7 0.7 convolution_bitcast_fusion
  229.4 0.0 copy-done.1
  229.4 0.1 copy.113
  229.5 0.6 gather_fusion.2
  230.2 3.0 %fusion.3 = f32[4,8,8,256]{3,2,1,0:T(8,128)S(1)} fusion(bf16[64,4,8,256]{3,0,2,1:T(8,128)(2,1)S(1)} %bitcast.101, bf16[4,8,256,256]{2,3,1,0:T(8,128)(2,1)} %get-tuple-element.9, f32[64,256,4]{1,2,0:T(4,128)S(1)} %convolution_bitcast_fusion), kind=kOutput, calls=%fused_computation.18 | convolution fusion | flops 268500992 | bytes 5767168 | tf_op jit(solution)/shard_map/jkib,cjkb->cji/dot_general | solution.py:71
  233.2 0.9 fusion.14
  (8 shorter events, 0.1 us)
Async XLA Ops:
  6.5 42.9 %all-gather.4.cloned.1.call-start = ((), (), s32[]{:S(2)}) async-start(), calls=%async_computation.2 | async-start | bytes 4718592 | tf_op jit(solution)/shard_map/all_gather | solution.py:24
  11.4 64.6 %all-to-all-start = ((s32[8,1,4]{2,1,0:T(1,128)}), s32[8,1,4]{2,1,0:T(1,128)S(1)}, u32[]{:S(2)}, u32[]{:S(2)}) async-start(s32[8,1,4]{2,1,0:T(1,128)} %copy.69), calls=%async_computation | async-start | bytes 8192 | tf_op jit(solution)/shard_map/all_to_all | solution.py:50
  49.4 5.0 %copy-start.2 = (bf16[1024,256]{1,0:T(8,128)(2,1)S(1)}, bf16[1024,256]{1,0:T(8,128)(2,1)}, u32[]{:S(2)}) copy-start(bf16[1024,256]{1,0:T(8,128)(2,1)} %fusion.9) | copy-start | bytes 1572868
  76.0 4.7 %copy-start.3 = (s32[1024]{0:T(1024)S(1)}, s32[1024]{0:T(1024)}, u32[]{:S(2)}) copy-start(s32[1024]{0:T(1024)} %param.7) | copy-start | bytes 12292
  76.0 87.0 %all-to-all-start.1 = ((bf16[8,4,256,256]{3,2,1,0:T(8,128)(2,1)}), bf16[8,4,256,256]{3,2,1,0:T(8,128)(2,1)}, u32[]{:S(2)}, u32[]{:S(2)}) async-start(bf16[8,4,256,256]{3,2,1,0:T(8,128)(2,1)} %copy.72), calls=%async_computation.1 | async-start | bytes 8388608 | tf_op jit(solution)/shard_map/all_to_all | solution.py:49
  80.6 108.8 %all-gather.6.cloned.1.call-start = ((), (), s32[]{:S(2)}) async-start(), calls=%async_computation.3 | async-start | bytes 1179648 | tf_op jit(solution)/shard_map/all_gather | solution.py:68
  166.8 56.7 %all-gather.8.cloned.1.call-start = ((), (), s32[]{:S(2)}) async-start(), calls=%async_computation.4 | async-start | bytes 1179648 | tf_op jit(solution)/shard_map/all_gather | solution.py:68
  191.3 4.0 %copy-start = (bf16[64,8192]{1,0:T(8,128)(2,1)S(1)}, bf16[64,8192]{1,0:T(8,128)(2,1)}, u32[]{:S(2)}) copy-start(bf16[64,8192]{1,0:T(8,128)(2,1)} %all-gather.6.cloned.1.call-done) | copy-start | bytes 3145732
  225.4 4.0 %copy-start.1 = (bf16[64,8192]{1,0:T(8,128)(2,1)S(1)}, bf16[64,8192]{1,0:T(8,128)(2,1)}, u32[]{:S(2)}) copy-start(bf16[64,8192]{1,0:T(8,128)(2,1)} %all-gather.8.cloned.1.call-done) | copy-start | bytes 3145732
Sparse Core Ops, SparseCore 0:
  10.0 39.4 all-gather.3
  166.9 22.4 all-gather.5
  200.0 23.4 all-gather.7
where the time goes:
time: 242 us; the launch traced here: 241 us
  blocking collectives  82 us (34%)
  waiting for transfers between devices  70.1 us (29%)
  local copies, waits for them, and re-layouts  30.6 us (13%)
  matrix products  25 us (10%)
  between operations  13.3 us (5%)
  starting transfers between devices  10.1 us (4%)
  other arithmetic  9.58 us (4%)
    psum x1, blocking collectives, local(): counts = lax.psum(jnp.sum(class_hits, axis=1), ('grp', 'row'))  82 us
    all_gather x2, waiting for transfers between devices, local(): group_spread = lax.all_gather(spread, 'row', axis=1, tiled=True)  46 us
    all_gather x1, waiting for transfers between devices, local(): group_units = lax.all_gather(unit_rows, 'row', axis=0, tiled=True)  24 us
    unnamed x10, local copies, waits for them, and re-layouts  8.82 us
    convert_element_type x1, local copies, waits for them, and re-layouts, local(): affinity_matrix = jnp.where(neighbour_tile_mask > 0, jnp.exp(score_values...  7.82 us
    dot_general x1, matrix products, local(): jnp.einsum('jie,jkbe->jkib', unit_rows.reshape(blocks_here, tile_edge, gr...  7.37 us
    dot_general x2, matrix products, local(): jnp.einsum('pjab,cpja->pjcb', mirrored, source_spread, preferred_element_...  6.55 us
    dot_general x2, matrix products, local(): jnp.einsum('jkib,cjkb->cji', affinity_matrix, column_spread, preferred_el...  6.05 us
  transfers between devices with their start and end apart: 5, of which 3 were waited for; matrix products, arithmetic and copies ran while one was open for 15% of the time, Pallas kernels for 0%

commit v1 on v0

v1 whole, which is shorter than its diff:
```python
import functools
import math

import jax
import jax.numpy as jnp
from jax import lax
from jax.experimental import pallas as pl
from jax.experimental.pallas import tpu as pltpu
from jax.sharding import PartitionSpec as P

CLASSES = 64
STEPS = 2


SOFTMAX_WARMTH = 0.1
PROPAGATION = 0.9

BF = jnp.bfloat16
F32 = jnp.float32
NT = (((1,), (1,)), ((), ()))


def peer_of(me, offset):
    peer, bit = me, 1
    while bit <= offset:
        if offset & bit:
            peer = peer + bit * (1 - 2 * lax.rem(lax.div(me, bit), 2))
        bit *= 2
    return peer


def gather_plan(n):
    if n != 8:
        first = [(0, d, d, c) for d in range(1, n) for c in range(2)]
        events = []
        for d in range(1, n):
            events += [("wait", d, 0, []), ("wait", d, 1, []), ("use", d)]
        return first, events
    first = [(0, 2, 2, 0), (0, 4, 4, 1), (0, 2, 2, 1), (0, 4, 4, 0), (0, 1, 1, 0), (0, 1, 1, 1)]
    events = [
        ("wait", 1, 0, []),
        ("wait", 1, 1, []),
        ("use", 1),
        ("wait", 2, 0, [(2, 6, 4, 0), (2, 3, 1, 0)]),
        ("wait", 4, 1, [(4, 6, 2, 1), (4, 5, 1, 1)]),
        ("wait", 2, 1, [(2, 3, 1, 1)]),
        ("wait", 4, 0, [(4, 5, 1, 0)]),
        ("use", 2),
        ("use", 4),
        ("wait", 6, 0, [(6, 7, 1, 0)]),
        ("wait", 6, 1, [(6, 7, 1, 1)]),
        ("wait", 3, 0, []),
        ("wait", 3, 1, []),
        ("use", 3),
        ("wait", 5, 0, []),
        ("wait", 5, 1, []),
        ("use", 5),
        ("use", 6),
        ("wait", 7, 0, []),
        ("wait", 7, 1, []),
        ("use", 7),
    ]
    return first, events


def kernel(n, groups, node_total, cb, emb, mask_hbm, labels, out, *scratch):
    scratch = list(scratch)
    take = lambda count: [scratch.pop(0) for _ in range(count)]
    units = take(n)
    spreads = [take(n) for _ in range(STEPS)]
    (mask, aff, rows, terms_out, terms_in, msg_out, msg_in, cnt_out, cnt_in) = take(9)
    (grp_out, grp_in, pick, seed, total) = take(5)
    (mask_sem, unit_s, unit_r, spread_s, spread_r, term_s, term_r) = take(7)
    (msg_s, msg_r, cnt_s, cnt_r, grp_s, grp_r) = take(6)
    J, K, T, _ = mask.shape
    E = emb.shape[1]
    C = CLASSES
    me = lax.axis_index("row")
    my_group = lax.axis_index("grp")
    peers = [peer_of(me, d) for d in range(n)]
    sent = []

    def remote(src, dst, send, recv, device):
        return pltpu.make_async_remote_copy(
            src_ref=src, dst_ref=dst, send_sem=send, recv_sem=recv, device_id=device,
            device_id_type=pl.DeviceIdType.MESH,
        )

    def start(copy):
        copy.start()
        sent.append(copy)

    mask_copies = [
        pltpu.make_async_copy(mask_hbm.at[j], mask.at[j], mask_sem.at[j]) for j in range(J)
    ]
    for copy in mask_copies:
        copy.start()
    barrier = pltpu.get_barrier_semaphore()
    for d in range(1, n):
        pl.semaphore_signal(
            barrier, inc=1, device_id={"row": peers[d]}, device_id_type=pl.DeviceIdType.MESH
        )
    others = [lax.rem(my_group + g, groups) for g in range(groups)]
    for g in range(1, groups):
        pl.semaphore_signal(
            barrier, inc=1, device_id={"grp": others[g]}, device_id_type=pl.DeviceIdType.MESH
        )

    def normalise(j, carry):
        features = emb[pl.ds(pl.multiple_of(j * T, T), T), :].astype(F32)
        mean = jnp.mean(features * features, axis=1, keepdims=True)
        units[0][j] = (features * lax.rsqrt(mean + 1e-06)).astype(BF)
        return carry

    lax.fori_loop(0, J, normalise, 0)
    pl.semaphore_wait(barrier, n - 1 + groups - 1)

    half = J // 2
    first, events = gather_plan(n)

    def gather_copy(slots, send, recv, move):
        src, dst, via, part = move
        piece = pl.ds(part * half, half)
        return remote(
            slots[src].at[piece], slots[dst].at[piece], send.at[dst, part], recv.at[dst, part],
            {"row": peers[via]},
        )

    def gather_start(slots, send, recv):
        for move in first:
            start(gather_copy(slots, send, recv, move))

    def gather_finish(slots, send, recv, use):
        for event in events:
            if event[0] == "use":
                use(event[1])
                continue
            _, slot, part, moves = event
            gather_copy(slots, send, recv, (0, slot, slot, part)).wait_recv()
            for move in moves:
                start(gather_copy(slots, send, recv, move))

    gather_start(units, unit_s, unit_r)

    wide = -(-C // 128) * 128
    ones_rows = jnp.ones((8, T), BF)
    count = jnp.zeros((8, wide), F32)
    for j in range(J):
        classes = lax.broadcasted_iota(jnp.int32, (wide, T), 0)
        hits = jnp.where(labels[:, j * T:(j + 1) * T] == classes, 1.0, 0.0).astype(BF)
        count += lax.dot_general(ones_rows, hits, NT, preferred_element_type=F32)
    cnt_out[...] = count
    cnt_copies = [None] + [
        remote(cnt_out, cnt_in.at[d], cnt_s.at[d], cnt_r.at[d], {"row": peers[d]})
        for d in range(1, n)
    ]
    for copy in cnt_copies[1:]:
        start(copy)

    def locate(j, d):
        slot, block, here = jnp.int32(0), jnp.int32(0), jnp.int32(0)
        base = peers[d] * J
        for k in range(K):
            at = cb[j, k] - base
            hit = jnp.logical_and(at >= 0, at < J)
            slot = jnp.where(hit, k, slot)
            block = jnp.where(hit, at, block)
            here = jnp.where(hit, 1, here)
        return slot, block, here

    lanes = lax.broadcasted_iota(jnp.int32, (8, J * C), 1)
    sublanes = lax.broadcasted_iota(jnp.int32, (8, T), 0)
    factor = math.log2(math.e) / (E * SOFTMAX_WARMTH)

    def tiles(d):
        def body(j, carry):
            column_sums, target_rows = carry
            slot, block, here = locate(j, d)
            score = lax.dot_general(
                units[0][j], units[d][block], NT, preferred_element_type=F32
            )
            tile = jnp.where(mask[j, slot] > 1 - here, jnp.exp2(score * factor), 0.0).astype(BF)
            aff[d, j] = tile
            row = lax.dot_general(ones_rows, tile, NT, preferred_element_type=F32)
            rows[j] = row if d == 0 else rows[j] + row
            column = jnp.dot(ones_rows, tile, preferred_element_type=F32)
            column_sums += jnp.where(sublanes == block, column, 0.0)
            inside = jnp.logical_and(lanes >= j * C, lanes < (j + 1) * C)
            target_rows = jnp.where(inside, lanes + (block - j) * C, target_rows)
            return column_sums, target_rows

        column_sums, target_rows = lax.fori_loop(
            0, J, body, (jnp.zeros((8, T), F32), jnp.zeros((8, J * C), jnp.int32))
        )
        own = msg_in if d == 0 else msg_out
        own[d, 0:8, 0:T] = column_sums
        own[d, 8:16, 0:J * C] = target_rows.astype(F32)
        if d:
            start(msg_copy(d))

    def msg_copy(d):
        return remote(msg_out.at[d], msg_in.at[d], msg_s.at[d], msg_r.at[d], {"row": peers[d]})

    for copy in mask_copies:
        copy.wait()
    tiles(0)

    for d in range(1, n):
        cnt_copies[d].wait_recv()
        count += cnt_in[d]
    grp_out[...] = count
    grp_copies = [
        remote(grp_out, grp_in.at[g], grp_s.at[g], grp_r.at[g], {"grp": others[g]})
        for g in range(1, groups)
    ]
    for copy in grp_copies:
        start(copy)

    gather_finish(units, unit_s, unit_r, tiles)

    for g in range(1, groups):
        grp_copies[g - 1].wait_recv()
        count += grp_in[g]
    weight = jnp.transpose(jnp.broadcast_to((node_total / (count + 1.0))[0:1, :], (wide, wide)))
    weight = weight[0:C, 0:1]
    for j in range(J):
        classes = lax.broadcasted_iota(jnp.int32, (C, T), 0)
        hits = jnp.where(labels[:, j * T:(j + 1) * T] == classes, 1.0, 0.0)
        seed[j] = hits * weight

    mirror_degree = msg_in[0, 0:8, 0:T]
    row_index = lax.broadcasted_iota(jnp.int32, (J * C, J * C), 0).astype(F32)
    for d in range(n):
        if d:
            msg_copy(d).wait_recv()
            mirror_degree += msg_in[d, 0:8, 0:T]
        pick[d] = jnp.where(row_index == msg_in[d, 8:9, 0:J * C], 1.0, 0.0).astype(BF)
    inverse_root = [
        lax.rsqrt(1.0 + rows[j][0:1, :] + mirror_degree[j:j + 1, :]) for j in range(J)
    ]

    order = sorted(range(1, n), reverse=True)
    for step in range(STEPS):
        slots = spreads[step]
        for j in range(J):
            field = seed[j] if step == 0 else total[j]
            slots[0][j] = (field * inverse_root[j]).astype(BF)
        gather_start(slots, spread_s.at[step], spread_r.at[step])

        def term_copy(d):
            return remote(
                terms_out.at[step, d], terms_in.at[step, d], term_s.at[step, d],
                term_r.at[step, d], {"row": peers[d]},
            )

        def mirror(d):
            for j in range(J):
                terms_out[step, d, j] = jnp.dot(
                    slots[0][j], aff[d, j], preferred_element_type=F32
                ).astype(BF)

        def forward(d):
            def body(j, carry):
                _, block, _ = locate(j, d)
                term = lax.dot_general(
                    slots[d][block], aff[d, j], NT, preferred_element_type=F32
                )
                total[j] = term if d == 0 else total[j] + term
                return carry

            lax.fori_loop(0, J, body, 0)

        for d in order:
            mirror(d)
            start(term_copy(d))
        mirror(0)
        forward(0)
        gather_finish(slots, spread_s.at[step], spread_r.at[step], forward)
        mirrored = jnp.dot(
            pick[0], terms_out[step, 0].reshape(J * C, T), preferred_element_type=F32
        )
        for d in range(1, n):
            term_copy(d).wait_recv()
            mirrored += jnp.dot(
                pick[d], terms_in[step, d].reshape(J * C, T), preferred_element_type=F32
            )
        for j in range(J):
            summed = total[j] + mirrored[j * C:(j + 1) * C, :] + slots[0][j].astype(F32)
            field = PROPAGATION * inverse_root[j] * summed + (1.0 - PROPAGATION) * seed[j]
            if step == STEPS - 1:
                out[:, j * T:(j + 1) * T] = field
            else:
                total[j] = field

    for copy in sent:
        copy.wait_send()


def local(embeddings, neighbour_tile_mask, column_blocks, seed_labels):
    J, K, T, _ = neighbour_tile_mask.shape
    E = embeddings.shape[1]
    C = CLASSES
    n = lax.axis_size("row")
    groups = lax.axis_size("grp")
    node_total = embeddings.shape[0] * n * groups
    wide = -(-C // 128) * 128
    width = max(T, J * C)
    dma = pltpu.SemaphoreType.DMA
    scratch = [pltpu.VMEM((J, T, E), BF) for _ in range(n)]
    scratch += [pltpu.VMEM((J, C, T), BF) for _ in range(n * STEPS)]
    scratch += [
        pltpu.VMEM((J, K, T, T), jnp.int32),
        pltpu.VMEM((n, J, T, T), BF),
        pltpu.VMEM((J, 8, T), F32),
        pltpu.VMEM((STEPS, n, J, C, T), BF),
        pltpu.VMEM((STEPS, n, J, C, T), BF),
        pltpu.VMEM((n, 16, width), F32),
        pltpu.VMEM((n, 16, width), F32),
        pltpu.VMEM((8, wide), F32),
        pltpu.VMEM((n, 8, wide), F32),
        pltpu.VMEM((8, wide), F32),
        pltpu.VMEM((groups, 8, wide), F32),
        pltpu.VMEM((n, J * C, J * C), BF),
        pltpu.VMEM((J, C, T), F32),
        pltpu.VMEM((J, C, T), F32),
        dma((J,)),
        dma((n, 2)), dma((n, 2)),
        dma((STEPS, n, 2)), dma((STEPS, n, 2)),
        dma((STEPS, n)), dma((STEPS, n)),
        dma((n,)), dma((n,)),
        dma((n,)), dma((n,)),
        dma((groups,)), dma((groups,)),
    ]
    vmem = pl.BlockSpec(memory_space=pltpu.VMEM)
    return pl.pallas_call(
        functools.partial(kernel, n, groups, node_total),
        out_shape=jax.ShapeDtypeStruct((C, J * T), F32),
        in_specs=[
            pl.BlockSpec(memory_space=pltpu.SMEM),
            vmem,
            pl.BlockSpec(memory_space=pl.ANY),
            vmem,
        ],
        out_specs=vmem,
        scratch_shapes=scratch,
        compiler_params=pltpu.CompilerParams(
            collective_id=0, has_side_effects=True, vmem_limit_bytes=56 * 1024 * 1024
        ),
    )(column_blocks, embeddings, neighbour_tile_mask, seed_labels.reshape(1, -1))


def solution(mesh):
    return jax.shard_map(
        local,
        mesh=mesh,
        in_specs=(
            P(("grp", "row"), None),
            P(("grp", "row"), None, None, None),
            P(("grp", "row"), None),
            P(("grp", "row")),
        ),
        out_specs=P(None, ("grp", "row")),
        check_vma=False,
    )
```

time: 242 us -> 85.6 us (0.35)
  Pallas kernels: 0 us -> 83.8 us
  blocking collectives: 82 us -> 0 us
  waiting for transfers between devices: 70.1 us -> 0 us
  local copies, waits for them, and re-layouts: 30.6 us -> 1.67 us
  matrix products: 25 us -> 0 us
  between operations: 13.3 us -> 0.01 us
  starting transfers between devices: 10.1 us -> 0 us
  other arithmetic: 9.58 us -> 0 us
    pallas_call x0 -> x1, Pallas kernels: none -> 83.8 us  [local(): pl.pallas_call(functools.partial(kernel, n, groups, node_total), out_shap...]
    psum x1 -> x0, blocking collectives: 82 us -> none  [local(): counts = lax.psum(jnp.sum(class_hits, axis=1), ('grp', 'row'))]
    all_gather x3 -> x0, waiting for transfers between devices: 70 us -> none  [the longest x2 46 us: local(): group_spread = lax.all_gather(spread, 'row', axis=1, tiled=True)]
    dot_general x9 -> x0, matrix products: 25 us -> none  [the longest x1 7.37 us: local(): jnp.einsum('jie,jkbe->jkib', unit_rows.reshape(blocks_here, tile_edge, gr...]
    convert_element_type x2 -> x0, local copies, waits for them, and re-layouts: 10.7 us -> none  [the longest x1 7.82 us: local(): affinity_matrix = jnp.where(neighbour_tile_mask > 0, jnp.exp(score_values...]
    all_to_all x2 -> x0, starting transfers between devices: 9.84 us -> none  [the longest x1 5.17 us: local(): lax.all_to_all(slot_target, 'row', split_axis=0, concat_axis=0, tiled=True)]
    unnamed x10 -> x1, local copies, waits for them, and re-layouts: 8.82 us -> 1.67 us
    gather x3 -> x0, local copies, waits for them, and re-layouts: 6.24 us -> none  [the longest x1 5.01 us: local(): column_units = group_units[column_blocks]]
  transfers between devices with their start and end apart: 5 -> 0, of which waited for: 3 -> 0; matrix products, arithmetic and copies ran while one was open for 15% -> 0% of each run, Pallas kernels for 0% -> 0%
where the time goes in v1:
time: 85.6 us; the launch traced here: 85.5 us
  Pallas kernels  83.8 us (98%)
  local copies, waits for them, and re-layouts  1.67 us (2%)
    pallas_call x1, Pallas kernels, local(): pl.pallas_call(functools.partial(kernel, n, groups, node_total), out_shap...  83.8 us

profile of v1, /device:TPU:0, one launch (start us, length us, event | category | flops | bytes accessed | tf_op | source)
XLA Modules:
  0.0 85.5 jit_solution(5992387167204059829)
XLA Ops:
  0.0 83.8 %shard_map.46 = f32[64,1024]{1,0:T(8,128)} custom-call(s32[4,8]{1,0:T(4,128)} %cb.1, bf16[1024,256]{1,0:T(8,128)(2,1)} %emb.1, s32[4,8,256,256]{3,2,1,0:T(8,128)} %mask_hbm.1, s32[1,1024]{1,0:T(1,128)} %bitcast.1), custom_call_target="tpu_custom_call" | custom-call | tf_op jit(solution)/shard_map/pallas_call | solution.py:335
  83.8 1.7 %copy.6 = f32[64,1024]{1,0:T(8,128)} copy(f32[64,1024]{1,0:T(8,128)} %shard_map.46) | data formatting | bytes 524288

commit v2 on v1

--- a/solution.py
+++ b/solution.py
@@ -40,11 +40,11 @@
     events = [
         ("wait", 1, 0, []),
         ("wait", 1, 1, []),
-        ("use", 1),
         ("wait", 2, 0, [(2, 6, 4, 0), (2, 3, 1, 0)]),
         ("wait", 4, 1, [(4, 6, 2, 1), (4, 5, 1, 1)]),
         ("wait", 2, 1, [(2, 3, 1, 1)]),
         ("wait", 4, 0, [(4, 5, 1, 0)]),
+        ("use", 1),
         ("use", 2),
         ("use", 4),
         ("wait", 6, 0, [(6, 7, 1, 0)]),
@@ -190,7 +190,8 @@
             return column_sums, target_rows
 
         column_sums, target_rows = lax.fori_loop(
-            0, J, body, (jnp.zeros((8, T), F32), jnp.zeros((8, J * C), jnp.int32))
+            0, J, body, (jnp.zeros((8, T), F32), jnp.zeros((8, J * C), jnp.int32)),
+            unroll=True,
         )
         own = msg_in if d == 0 else msg_out
         own[d, 0:8, 0:T] = column_sums
@@ -268,14 +269,19 @@
                 total[j] = term if d == 0 else total[j] + term
                 return carry
 
-            lax.fori_loop(0, J, body, 0)
+            lax.fori_loop(0, J, body, 0, unroll=True)
 
         for d in order:
             mirror(d)
             start(term_copy(d))
-        mirror(0)
-        forward(0)
-        gather_finish(slots, spread_s.at[step], spread_r.at[step], forward)
+
+        def use(d):
+            if d == 1:
+                mirror(0)
+                forward(0)
+            forward(d)
+
+        gather_finish(slots, spread_s.at[step], spread_r.at[step], use)
         mirrored = jnp.dot(
             pick[0], terms_out[step, 0].reshape(J * C, T), preferred_element_type=F32
         )

time: 85.6 us -> 78.1 us (0.912)
  Pallas kernels: 83.8 us -> 76 us
    pallas_call x1, Pallas kernels: 83.8 us -> 76 us  [local(): pl.pallas_call(functools.partial(kernel, n, groups, node_total), out_shap...]
where the time goes in v2:
time: 78.1 us; the launch traced here: 77.7 us
  Pallas kernels  76 us (97%)
  local copies, waits for them, and re-layouts  1.67 us (2%)
    pallas_call x1, Pallas kernels, local(): pl.pallas_call(functools.partial(kernel, n, groups, node_total), out_shap...  76 us
    unnamed x1, local copies, waits for them, and re-layouts  1.67 us

profile of v2, /device:TPU:0, one launch (start us, length us, event | category | flops | bytes accessed | tf_op | source)
XLA Modules:
  0.0 77.7 jit_solution(13101131024938481318)
XLA Ops:
  0.0 76.0 %shard_map.46 = f32[64,1024]{1,0:T(8,128)} custom-call(s32[4,8]{1,0:T(4,128)} %cb.1, bf16[1024,256]{1,0:T(8,128)(2,1)} %emb.1, s32[4,8,256,256]{3,2,1,0:T(8,128)} %mask_hbm.1, s32[1,1024]{1,0:T(1,128)} %bitcast.1), custom_call_target="tpu_custom_call" | custom-call | tf_op jit(solution)/shard_map/pallas_call | solution.py:341
  76.0 1.7 %copy.6 = f32[64,1024]{1,0:T(8,128)} copy(f32[64,1024]{1,0:T(8,128)} %shard_map.46) | data formatting | bytes 524288
